TPU v7x, 256 devices: a whole 4x4x8 slice. The times are simulated.
256 devices in a mesh: energy: 64 (over y, z, x_hi), slab: 4 (over x_lo, core).
Axes of the slice: x: 4 (x_hi: 2, x_lo: 2; x = x_hi * 2 + x_lo), y: 4, z: 8, core: 2. Of those that a mesh axis runs over, the one named last changes fastest.
Arguments:
- lesser: bfloat16 [64, 4, 2, 1024, 1024], P('energy', 'slab'), may hold values from -6 to 6
- greater_diag: float32 [64, 4, 1024], P('energy', 'slab'), may hold values from -6 to 6
- dipole: bfloat16 [4, 1024, 1024], P('slab'), may hold values from -0.1875 to 0.1875
- photon_weights: float32 [64, 3], P('energy'), may hold values from 0.2 to 1
- sidebands: int32 [64], P('energy'), may hold values from 1 to 2
- phonon_lags: int32 [6], replicated, may hold values from 1 to 31
- phonon_strengths: float32 [2, 6], replicated, may hold values from 0.3 to 1.5
- slab_coupling: float32 [4, 1024], P('slab'), may hold values from 0.3 to 1
Outputs:
- lesser_self: bfloat16 [64, 4, 2, 1024, 1024], P('energy', 'slab')
- greater_phonon: float32 [64, 4, 1024], P('energy', 'slab')
All inputs are finite; a program needn't handle non-finite values.
Results may differ from a plain program's by a relative error of at most 0.0057.
Values may be sent and summed in bfloat16 or wider, within the bound.
A program may use at most 64 MiB of HBM per device.

v0:
```python
import jax
import jax.numpy as jnp
from jax import lax
from jax.sharding import PartitionSpec as P

PHOT_BLOCKS = 3


def extended(block, sides, width):
    for axis, dim in sides:
        count = lax.axis_size(axis)
        forward = [(i, i + 1) for i in range(count - 1)]
        backward = [(target, source) for source, target in forward]
        low = lax.ppermute(
            lax.slice_in_dim(block, block.shape[dim] - width, None, axis=dim), axis, forward
        )
        high = lax.ppermute(lax.slice_in_dim(block, 0, width, axis=dim), axis, backward)
        block = jnp.concatenate([low, block, high], axis=dim)
    return block


def shifted(block, axis, distance):
    devices = range(lax.axis_size(axis))
    route = [(i - distance, i) for i in devices if i - distance in devices]
    return lax.ppermute(block, axis, route)


def kernel(rows, cols, phonon_lags, first, second):
    offset = cols[None, :] - rows[:, None]
    upward = (offset[None, :, :] == phonon_lags[:, None, None]).astype(jnp.float32)
    downward = (offset[None, :, :] == -phonon_lags[:, None, None]).astype(jnp.float32)
    return jnp.sum(first[:, None, None] * upward + second[:, None, None] * downward, axis=0)


def left_of(blocks, dipole):
    return jnp.einsum(
        "escij,skj->escik", blocks, dipole, preferred_element_type=jnp.float32
    ).astype(jnp.bfloat16)


def on_device(
    lesser,
    greater_diag,
    dipole,
    photon_weights,
    sidebands,
    phonon_lags,
    phonon_strengths,
    slab_coupling,
):
    e_count = lesser.shape[0]
    width = lesser.shape[-1]
    total_e = e_count * lax.axis_size("energy")
    own_rows = lax.axis_index("energy") * e_count + jnp.arange(e_count, dtype=jnp.int32)
    diag_less = jnp.diagonal(lesser[:, :, 1], axis1=-2, axis2=-1).astype(jnp.float32)
    stacked_diag = jnp.concatenate([diag_less, greater_diag], axis=-1)
    everyone = lax.all_gather(stacked_diag, "energy", axis=0, tiled=True)
    all_rows = jnp.arange(total_e, dtype=jnp.int32)
    k_less = kernel(own_rows, all_rows, phonon_lags, phonon_strengths[0], phonon_strengths[1])
    k_great = kernel(own_rows, all_rows, phonon_lags, phonon_strengths[1], phonon_strengths[0])
    corr_less = jnp.einsum(
        "ef,fsn->esn", k_less, everyone[..., :width], precision=lax.Precision.HIGHEST
    )
    corr_great = jnp.einsum(
        "ef,fsn->esn", k_great, everyone[..., width:], precision=lax.Precision.HIGHEST
    )
    correlated = jnp.concatenate([corr_less, corr_great], axis=-1)
    coupling = jnp.concatenate([slab_coupling, slab_coupling], axis=-1)
    outgoing = jnp.stack([correlated, coupling * correlated])
    rims = extended(outgoing, (("slab", 2),), 1)
    phonon = correlated + rims[1, :, 0:1] + coupling * rims[0, :, 2:3]
    own_left = left_of(lesser, dipole)
    lower = shifted(own_left, "energy", PHOT_BLOCKS)
    upper = shifted(own_left, "energy", -PHOT_BLOCKS)
    weights = photon_weights[:, :, None, None, None, None]
    flags = sidebands.astype(jnp.float32)[:, None, None, None, None]
    mixed = (
        weights[:, 0] * own_left.astype(jnp.float32)
        + flags
        * (weights[:, 1] * lower.astype(jnp.float32) + weights[:, 2] * upper.astype(jnp.float32))
    ).astype(jnp.bfloat16)
    photon = jnp.einsum("sij,escjk->escik", dipole, mixed, preferred_element_type=jnp.float32)
    eye_mask = (jnp.arange(width)[:, None] == jnp.arange(width)[None, :]).astype(jnp.float32)
    photon = photon.at[:, :, 1].add(eye_mask * phonon[..., :width, None])
    return (photon.astype(jnp.bfloat16), phonon[..., width:])


def solution(mesh):
    return jax.shard_map(
        on_device,
        mesh=mesh,
        in_specs=(
            P("energy", "slab", None, None, None),
            P("energy", "slab", None),
            P("slab", None, None),
            P("energy", None),
            P("energy"),
            P(),
            P(),
            P("slab", None),
        ),
        out_specs=(P("energy", "slab", None, None, None), P("energy", "slab", None)),
        check_vma=False,
    )
```

profile of v0, /device:TPU:1, one launch (start us, length us, event | category | flops | bytes accessed | tf_op | source)
XLA Modules:
  0.0 408.2 jit_solution(17339647209610599391)
XLA Ops:
  0.6 0.0 copy-start
  0.6 0.0 copy-start.5
  0.7 1.6 copy-done
  2.2 8.3 %convert_bitcast_fusion = bf16[1,1,2,1024,1024]{3,4,2,0,1:T(8,128)(2,1)} fusion(bf16[1,1,2,1024,1024]{4,3,2,1,0:T(8,128)(2,1)} %param.10, bf16[1,1024,1024]{2,1,0:T(8,128)(2,1)S(1)} %copy-done), kind=kOutput, calls=%fused_computation.13 | convolution fusion | flops 4297064448 | bytes 10485760 | tf_op jit(solution)/shard_map/escij,skj->escik/dot_general | solution.py:36
  10.5 0.0 copy-start.1
  10.5 1.4 collective-permute-start.1
  11.9 9.4 %collective-permute-start = (bf16[1,1,2,1024,1024]{3,4,2,0,1:T(8,128)(2,1)}, bf16[1,1,2,1024,1024]{3,4,2,0,1:T(8,128)(2,1)}, u32[]{:S(2)}, u32[]{:S(2)}) collective-permute-start(bf16[1,1,2,1024,1024]{3,4,2,0,1:T(8,128)(2,1)} %convert_bitcast_fusion), channel_id=1, source_target_pairs={{0,12},{4,16},{8,20},{12,24},{16,28},{20,32},{24,36},{28,40},{32,4... | collective-permute-start | bytes 12582920 | tf_op jit(solution)/shard_map/ppermute | solution.py:25
  21.4 0.0 copy-done.5
  21.4 0.0 copy-start.2
  21.4 3.1 slice_bitcast_fusion.1
  24.5 16.3 %gather_fusion = bf16[1024]{0:T(1024)(128)(2,1)S(1)} fusion(bf16[1024,1024]{1,0:T(8,128)(2,1)} %slice_bitcast_fusion.1, s32[1024]{0:T(1024)S(1)} %bitcast.83), kind=kCustom, calls=%fused_computation | custom fusion | bytes 12288 | tf_op jit(solution)/shard_map/jit(diagonal)/gather | solution.py:55
  40.8 0.0 copy-done.1
  40.9 0.0 copy-done.4
  40.9 0.1 fusion.27
  41.0 0.0 copy-done.3
  41.0 305.5 %all_gather.3 = f32[64,1,2048]{2,1,0:T(1,128)S(1)} all-gather(f32[1,1,2048]{2,1,0:T(1,128)S(1)} %pad_maximum_fusion.1), channel_id=1, replica_groups=mesh['energy'=64,'slab'=4] {'energy'}, dimensions={0}, use_global_device_ids=true | all-gather | bytes 532480 | tf_op jit(solution)/shard_map/all_gather | solution.py:57
  346.6 0.3 fusion.18
  346.8 0.3 fusion.15
  347.2 35.3 %collective-permute-start.3 = (f32[2,1,1,2048]{3,2,1,0:T(1,128)S(1)}, f32[2,1,1,2048]{3,2,1,0:T(1,128)S(1)}, u32[]{:S(2)}, u32[]{:S(2)}) collective-permute-start(f32[2,1,1,2048]{3,2,1,0:T(1,128)S(1)} %pad_maximum_fusion), channel_id=1, source_target_pairs={{1,0},{2,1},{3,2},{5,4},{6,5},{7,6},{9,8},{10,9},{11,10},{13,12},{... | collective-permute-start | bytes 49160 | tf_op jit(solution)/shard_map/ppermute | solution.py:17
  382.5 2.6 collective-permute-start.2
  385.1 0.0 copy-done.2
  385.2 0.6 fusion.33
  386.4 0.0 collective-permute-done.3
  386.5 0.0 collective-permute-done.2
  386.5 0.6 fusion.32
  387.1 0.0 collective-permute-done.1
  387.1 0.0 collective-permute-done
  387.1 10.0 %fusion.1 = f32[2,1024,1024]{2,1,0:T(8,128)S(1)} fusion(bf16[1,1,2,1024,1024]{3,4,2,0,1:T(8,128)(2,1)} %collective-permute-done.1, bf16[1,1,2,1024,1024]{3,4,2,0,1:T(8,128)(2,1)} %collective-permute-done, bf16[1,1,2,1024,1024]{3,4,2,0,1:T(8,128)(2,1)} %convert_bitcast_fusion, f32[]{:T(128)} %bitcast.10, f32[]{:T(128)} %bitcast.8, f32[]{:T(128)} %bitcast.7, ...), kind=kOutput, calls=%fused_computation.3 | convolution fusion | flops 4315938816 | bytes 23068688 | tf_op jit(solution)/shard_map/sij,escjk->escik/dot_general | solution.py:82
  397.1 1.7 copy.25
  398.7 0.7 fusion.4
  399.4 2.6 convert_element_type.53
  402.0 6.2 %copy.13 = bf16[1,1,2,1024,1024]{4,3,2,1,0:T(8,128)(2,1)} copy(bf16[1,1,2,1024,1024]{3,4,2,0,1:T(8,128)(2,1)} %convert_element_type.53) | data formatting | bytes 8388608
  (15 shorter events, 0.2 us)
Async XLA Ops:
  0.6 1.6 copy-start
  0.6 20.7 %copy-start.5 = (s32[6]{0:T(128)S(1)}, s32[6]{0:T(128)}, u32[]{:S(2)}) copy-start(s32[6]{0:T(128)} %param.15) | copy-start | bytes 76
  10.5 30.4 %copy-start.1 = (f32[1,1024]{1,0:T(1,128)S(1)}, f32[1,1024]{1,0:T(1,128)}, u32[]{:S(2)}) copy-start(f32[1,1024]{1,0:T(1,128)} %param.17) | copy-start | bytes 12292
  10.5 30.4 %copy-start.4 = (f32[2,6]{1,0:T(2,128)S(1)}, f32[2,6]{1,0:T(2,128)}, u32[]{:S(2)}) copy-start(f32[2,6]{1,0:T(2,128)} %param.16) | copy-start | bytes 148
  10.5 30.5 %copy-start.3 = (f32[1,1,1024]{2,1,0:T(1,128)S(1)}, f32[1,1,1024]{2,1,0:T(1,128)}, u32[]{:S(2)}) copy-start(f32[1,1,1024]{2,1,0:T(1,128)} %param.11) | copy-start | bytes 12292
  10.5 376.6 %collective-permute-start.1 = (bf16[1,1,2,1024,1024]{3,4,2,0,1:T(8,128)(2,1)}, bf16[1,1,2,1024,1024]{3,4,2,0,1:T(8,128)(2,1)}, u32[]{:S(2)}, u32[]{:S(2)}) collective-permute-start(bf16[1,1,2,1024,1024]{3,4,2,0,1:T(8,128)(2,1)} %convert_bitcast_fusion), channel_id=1, source_target_pairs={{12,0},{16,4},{20,8},{24,12},{28,16},{32,20},{36,24},{40,28},{44,3... | collective-permute-start | bytes 12582920 | tf_op jit(solution)/shard_map/ppermute | solution.py:25
  11.9 375.2 %collective-permute-start = (bf16[1,1,2,1024,1024]{3,4,2,0,1:T(8,128)(2,1)}, bf16[1,1,2,1024,1024]{3,4,2,0,1:T(8,128)(2,1)}, u32[]{:S(2)}, u32[]{:S(2)}) collective-permute-start(bf16[1,1,2,1024,1024]{3,4,2,0,1:T(8,128)(2,1)} %convert_bitcast_fusion), channel_id=1, source_target_pairs={{0,12},{4,16},{8,20},{12,24},{16,28},{20,32},{24,36},{28,40},{32,4... | collective-permute-start | bytes 12582920 | tf_op jit(solution)/shard_map/ppermute | solution.py:25
  21.4 363.8 %copy-start.2 = (f32[1,3]{1,0:T(1,128)S(1)}, f32[1,3]{1,0:T(1,128)}, u32[]{:S(2)}) copy-start(f32[1,3]{1,0:T(1,128)} %param.13) | copy-start | bytes 40
  347.2 39.3 %collective-permute-start.3 = (f32[2,1,1,2048]{3,2,1,0:T(1,128)S(1)}, f32[2,1,1,2048]{3,2,1,0:T(1,128)S(1)}, u32[]{:S(2)}, u32[]{:S(2)}) collective-permute-start(f32[2,1,1,2048]{3,2,1,0:T(1,128)S(1)} %pad_maximum_fusion), channel_id=1, source_target_pairs={{1,0},{2,1},{3,2},{5,4},{6,5},{7,6},{9,8},{10,9},{11,10},{13,12},{... | collective-permute-start | bytes 49160 | tf_op jit(solution)/shard_map/ppermute | solution.py:17
  382.5 4.0 collective-permute-start.2
where the time goes:
time: 409 us; the launch traced here: 408 us
  blocking collectives  306 us (75%)
  starting transfers between devices  48.8 us (12%)
  local copies, waits for them, and re-layouts  30.2 us (7%)
  matrix products  18.8 us (5%)
    all_gather x1, blocking collectives, on_device(): everyone = lax.all_gather(stacked_diag, 'energy', axis=0, tiled=True)  306 us
    ppermute x1, starting transfers between devices, extended(): lax.ppermute(lax.slice_in_dim(block, 0, width, axis=dim), axis, backward)  35.3 us
    gather x1, local copies, waits for them, and re-layouts, on_device(): jnp.diagonal(lesser[:, :, 1], axis1=-2, axis2=-1).astype(jnp.float32)  16.3 us
    ppermute x2, starting transfers between devices, shifted(): return lax.ppermute(block, axis, route)  10.9 us
    dot_general x1, matrix products, on_device(): jnp.einsum('sij,escjk->escik', dipole, mixed, preferred_element_type=jnp....  9.97 us
    unnamed x15, local copies, waits for them, and re-layouts  9.44 us
    dot_general x1, matrix products, left_of(): jnp.einsum('escij,skj->escik', blocks, dipole, preferred_element_type=jnp...  8.26 us
  transfers between devices with their start and end apart: 4, of which 0 were waited for; matrix products, arithmetic and copies ran while one was open for 5% of the time, Pallas kernels for 0%

commit v1 on v0

v1 whole, which is shorter than its diff:
```python
import jax
import jax.numpy as jnp
from jax import lax
from jax.experimental import pallas as pl
from jax.experimental.pallas import tpu as pltpu
from jax.sharding import PartitionSpec as P

F32, BF16 = jnp.float32, jnp.bfloat16
MESH = pl.DeviceIdType.MESH

RING = 8
LAYERS = 4
CHAIN = RING * LAYERS
SLABS = 4
MODES = 6
NORB = 1024
ROWS = 128
CHUNKS = NORB // ROWS
LAG = 2
BLOCK = 256
LANE = 128

CROSS, LOW, HIGH, BLOW, BHIGH, SUMS = range(6)


def body(
    lesser, great, dip, weights, flags, lags, strengths, coupling,
    out, great_out,
    g_v, d_v, crossed, low, high, blow, bhigh, sums, sums_out, left, acc, stage,
    zbuf, pbuf, qbuf, nbuf, nsend, phon, wsend, wrecv,
    send, recv, zs, zr, ps, pr, ns, nr, ws, wr, local, osem,
):
    e = lax.axis_index("energy")
    s = lax.axis_index("slab")
    w, h = e // 2, e % 2
    y, z = w // RING, w % RING
    mirror = (w * 2 + (1 - h), s)

    def at(chain):
        return (chain * 2 + h, s)

    def inside(chain):
        return jnp.logical_and(chain >= 0, chain < CHAIN)

    a_low, a_high = h - 2, h + 1
    b_low, b_high = -1 - h, 2 - h

    copies_in = [
        pltpu.make_async_copy(lesser.at[1], g_v.at[1], local.at[0]),
        pltpu.make_async_copy(lesser.at[0], g_v.at[0], local.at[1]),
        pltpu.make_async_copy(dip, d_v, local.at[2]),
    ]
    for copy in copies_in:
        copy.start()

    barrier = pltpu.get_barrier_semaphore()
    expected = jnp.int32(2 * (RING - 1))
    for step in (-2, -1, 1, 2):
        ok = inside(w + step)
        expected = expected + ok.astype(jnp.int32)

        @pl.when(ok)
        def _():
            pl.semaphore_signal(barrier, inc=1, device_id=at(w + step), device_id_type=MESH)

    def ring_mate(d):
        return ((y * RING + (z + d) % RING) * 2 + h, s)

    def plane_mate(t):
        return ((((y + t // 2) % LAYERS) * RING + z) * 2 + (h + t % 2) % 2, s)

    for d in range(1, RING):
        pl.semaphore_signal(barrier, inc=1, device_id=ring_mate(d), device_id_type=MESH)
        pl.semaphore_signal(barrier, inc=1, device_id=plane_mate(d), device_id_type=MESH)
    for step in (-1, 1):
        ok = jnp.logical_and(s + step >= 0, s + step < SLABS)
        expected = expected + ok.astype(jnp.int32)

        @pl.when(ok)
        def _():
            pl.semaphore_signal(barrier, inc=1, device_id=(e, s + step), device_id_type=MESH)

    pl.semaphore_wait(barrier, expected)

    def chunk_copy(stream, k):
        source, target, device = {
            CROSS: (lesser.at[0, pl.ds(k * ROWS, ROWS)], crossed.at[k], mirror),
            LOW: (crossed.at[k], low.at[k], at(w - a_low)),
            HIGH: (crossed.at[k], high.at[k], at(w - a_high)),
            BLOW: (lesser.at[1, pl.ds(k * ROWS, ROWS)], blow.at[k], at(w - b_low)),
            BHIGH: (lesser.at[1, pl.ds(k * ROWS, ROWS)], bhigh.at[k], at(w - b_high)),
            SUMS: (sums_out.at[k], sums.at[k], mirror),
        }[stream]
        return pltpu.make_async_remote_copy(
            source, target, send.at[stream, k], recv.at[stream, k],
            device_id=device, device_id_type=MESH,
        )

    sends_to = {
        LOW: inside(w - a_low), HIGH: inside(w - a_high),
        BLOW: inside(w - b_low), BHIGH: inside(w - b_high),
    }
    hears = {
        LOW: inside(w + a_low), HIGH: inside(w + a_high),
        BLOW: inside(w + b_low), BHIGH: inside(w + b_high),
    }

    def start(stream, k):
        if stream in sends_to:

            @pl.when(sends_to[stream])
            def _():
                chunk_copy(stream, k).start()
        else:
            chunk_copy(stream, k).start()

    def arrive(stream, k):
        if stream in hears:

            @pl.when(hears[stream])
            def _():
                chunk_copy(stream, k).wait_recv()
        else:
            chunk_copy(stream, k).wait_recv()

    def sent(stream, k):
        if stream in sends_to:

            @pl.when(sends_to[stream])
            def _():
                chunk_copy(stream, k).wait_send()
        else:
            chunk_copy(stream, k).wait_send()

    flag = flags[0].astype(F32)
    own_w, low_w, high_w = weights[0, 0], flag * weights[0, 1], flag * weights[0, 2]
    wsend[0] = jnp.full((8, LANE), low_w, F32)
    wsend[1] = jnp.full((8, LANE), high_w, F32)
    weight_copy = pltpu.make_async_remote_copy(
        wsend, wrecv, ws, wr, device_id=mirror, device_id_type=MESH
    )
    weight_copy.start()

    @pl.loop(0, CHUNKS)
    def _(k):
        start(BHIGH, k)
        start(BLOW, k)
        start(CROSS, k)

    for stream, buffer in ((LOW, low), (HIGH, high), (BLOW, blow), (BHIGH, bhigh)):

        @pl.when(jnp.logical_not(hears[stream]))
        def _():
            @pl.loop(0, CHUNKS)
            def _(k):
                buffer[k] = jnp.zeros((ROWS, NORB), BF16)

    eye = lax.broadcasted_iota(jnp.int32, (LANE, LANE), 0) == lax.broadcasted_iota(
        jnp.int32, (LANE, LANE), 1
    )
    copies_in[0].wait()
    for b in range(NORB // LANE):
        part = slice(b * LANE, (b + 1) * LANE)
        tile = jnp.where(eye, g_v[1, part, part].astype(F32), 0.0)
        zbuf[0, b : b + 1, :] = jnp.sum(tile, axis=0, keepdims=True)
    zbuf[0, 8:16, :] = great[...]

    def ring_copy(d):
        return pltpu.make_async_remote_copy(
            zbuf.at[0], zbuf.at[d], zs.at[d], zr.at[d],
            device_id=ring_mate(d), device_id_type=MESH,
        )

    for d in range(1, RING):
        ring_copy(d).start()

    for c in range(2):

        @pl.loop(0, NORB // BLOCK)
        def _(i):
            acc[c, pl.ds(i * BLOCK, BLOCK), :] = jnp.zeros((BLOCK, NORB), F32)

    copies_in[1].wait()
    copies_in[2].wait()
    weight_copy.wait()
    m_low, m_high = wrecv[0, 0:1, 0:1], wrecv[1, 0:1, 0:1]

    def plane_copy(t):
        return pltpu.make_async_remote_copy(
            pbuf.at[t], qbuf.at[t], ps.at[t], pr.at[t],
            device_id=plane_mate(t), device_id_type=MESH,
        )

    def partial_sums():
        for d in range(1, RING):
            ring_copy(d).wait()

        @pl.loop(0, RING)
        def _(t):
            row = (((y + t // 2) % LAYERS) * RING + z) * 2 + (h + t % 2) % 2
            less = jnp.zeros((8, LANE), F32)
            more = jnp.zeros((8, LANE), F32)
            for d in range(RING):
                column = (y * RING + (z - d + RING) % RING) * 2 + h
                k_less = jnp.float32(0.0)
                k_great = jnp.float32(0.0)
                for m in range(MODES):
                    up = column - row == lags[m]
                    down = row - column == lags[m]
                    first, second = strengths[0, m], strengths[1, m]
                    k_less += jnp.where(up, first, 0.0) + jnp.where(down, second, 0.0)
                    k_great += jnp.where(up, second, 0.0) + jnp.where(down, first, 0.0)
                less += k_less * zbuf[d, 0:8, :]
                more += k_great * zbuf[d, 8:16, :]
            pbuf[t, 0:8, :] = less
            pbuf[t, 8:16, :] = more

        for t in range(1, RING):
            plane_copy(t).start()

    def neighbour_copy(side):
        return pltpu.make_async_remote_copy(
            nsend.at[side], nbuf.at[side], ns.at[side], nr.at[side],
            device_id=(e, s + 1 - 2 * side), device_id_type=MESH,
        )

    goes_up, goes_down = s + 1 < SLABS, s > 0

    def correlate():
        total = pbuf[0]
        for t in range(1, RING):
            plane_copy(t).wait()
            total += qbuf[t]
        nsend[1] = total
        for part in (slice(0, 8), slice(8, 16)):
            nsend[0, part, :] = coupling[...] * total[part, :]

        @pl.when(goes_up)
        def _():
            neighbour_copy(0).start()

        @pl.when(goes_down)
        def _():
            neighbour_copy(1).start()

        @pl.when(jnp.logical_not(goes_down))
        def _():
            nbuf[0] = jnp.zeros((16, LANE), F32)

        @pl.when(jnp.logical_not(goes_up))
        def _():
            nbuf[1] = jnp.zeros((16, LANE), F32)

    def couple():
        @pl.when(goes_up)
        def _():
            neighbour_copy(0).wait_send()
            neighbour_copy(1).wait_recv()

        @pl.when(goes_down)
        def _():
            neighbour_copy(1).wait_send()
            neighbour_copy(0).wait_recv()

        for part in (slice(0, 8), slice(8, 16)):
            phon[part, :] = nsend[1, part, :] + nbuf[0, part, :] + coupling[...] * nbuf[1, part, :]
        great_out[...] = phon[8:16, :]

    def multiply(c, k, mixed):
        left[c] = lax.dot_general(
            mixed, d_v[...], (((1,), (1,)), ((), ())), preferred_element_type=F32
        ).astype(BF16)
        columns = pl.ds(pl.multiple_of(k * ROWS, ROWS), ROWS)

        @pl.loop(0, NORB // BLOCK)
        def _(i):
            rows = pl.ds(pl.multiple_of(i * BLOCK, BLOCK), BLOCK)
            acc[c, rows, :] += jnp.dot(d_v[rows, columns], left[c], preferred_element_type=F32)

    def own(c, k):
        return own_w * g_v[c, pl.ds(k * ROWS, ROWS), :].astype(F32)

    @pl.loop(0, CHUNKS + LAG)
    def _(k):
        @pl.when(k < CHUNKS)
        def _():
            arrive(CROSS, k)
            start(LOW, k)
            start(HIGH, k)
            arrive(BLOW, k)
            arrive(BHIGH, k)
            sums_out[k] = (m_low * blow[k].astype(F32) + m_high * bhigh[k].astype(F32)).astype(BF16)
            start(SUMS, k)

        @pl.when(k == 2)
        def _():
            partial_sums()

        @pl.when(k == 4)
        def _():
            correlate()

        @pl.when(k == 6)
        def _():
            couple()

        @pl.when(k >= LAG)
        def _():
            j = k - LAG
            arrive(SUMS, j)
            multiply(1, j, (own(1, j) + sums[j].astype(F32)).astype(BF16))

    def write(c):
        return pltpu.make_async_copy(stage.at[c], out.at[c], osem.at[c])

    def finish(c):
        for i in range(NORB // LANE):
            rows = slice(i * LANE, (i + 1) * LANE)
            stage[c, rows, :] = acc[c, rows, :].astype(BF16)
            if c == 1:
                stage[1, rows, rows] = (
                    acc[1, rows, rows] + jnp.where(eye, phon[i : i + 1, :], 0.0)
                ).astype(BF16)
        write(c).start()

    finish(1)

    @pl.loop(0, CHUNKS)
    def _(k):
        arrive(LOW, k)
        arrive(HIGH, k)
        mixed = own(0, k) + low_w * low[k].astype(F32) + high_w * high[k].astype(F32)
        multiply(0, k, mixed.astype(BF16))

    finish(0)

    @pl.loop(0, CHUNKS)
    def _(k):
        for stream in (CROSS, LOW, HIGH, BLOW, BHIGH, SUMS):
            sent(stream, k)

    write(1).wait()
    write(0).wait()


def on_device(lesser, great, dipole, weights, flags, lags, strengths, coupling):
    vmem = pl.BlockSpec(memory_space=pltpu.VMEM)
    smem = pl.BlockSpec(memory_space=pltpu.SMEM)
    hbm = pl.BlockSpec(memory_space=pl.ANY)
    chunks = pltpu.VMEM((CHUNKS, ROWS, NORB), BF16)
    dma = pltpu.SemaphoreType.DMA
    out, great_out = pl.pallas_call(
        body,
        out_shape=(
            jax.ShapeDtypeStruct((2, NORB, NORB), BF16),
            jax.ShapeDtypeStruct((8, LANE), F32),
        ),
        in_specs=[hbm, vmem, hbm, smem, smem, smem, smem, vmem],
        out_specs=(hbm, vmem),
        scratch_shapes=[
            pltpu.VMEM((2, NORB, NORB), BF16),
            pltpu.VMEM((NORB, NORB), BF16),
            chunks, chunks, chunks, chunks, chunks, chunks, chunks,
            pltpu.VMEM((2, ROWS, NORB), BF16),
            pltpu.VMEM((2, NORB, NORB), F32),
            pltpu.VMEM((2, NORB, NORB), BF16),
            pltpu.VMEM((RING, 16, LANE), F32),
            pltpu.VMEM((RING, 16, LANE), F32),
            pltpu.VMEM((RING, 16, LANE), F32),
            pltpu.VMEM((2, 16, LANE), F32),
            pltpu.VMEM((2, 16, LANE), F32),
            pltpu.VMEM((16, LANE), F32),
            pltpu.VMEM((2, 8, LANE), F32),
            pltpu.VMEM((2, 8, LANE), F32),
            dma((6, CHUNKS)), dma((6, CHUNKS)),
            dma((RING,)), dma((RING,)),
            dma((RING,)), dma((RING,)),
            dma((2,)), dma((2,)),
            dma, dma,
            dma((3,)), dma((2,)),
        ],
        name="stencil",
        cost_estimate=pl.CostEstimate(
            flops=8 * NORB**3, bytes_accessed=10 * NORB * NORB, transcendentals=0
        ),
        compiler_params=pltpu.CompilerParams(
            collective_id=0, has_side_effects=True, vmem_limit_bytes=56 << 20
        ),
    )(
        lesser.reshape(2, NORB, NORB), great.reshape(8, LANE), dipole.reshape(NORB, NORB),
        weights, flags, lags, strengths, coupling.reshape(8, LANE),
    )
    return out.reshape(1, 1, 2, NORB, NORB), great_out.reshape(1, 1, NORB)


def solution(mesh):
    return jax.shard_map(
        on_device,
        mesh=mesh,
        in_specs=(
            P("energy", "slab", None, None, None),
            P("energy", "slab", None),
            P("slab", None, None),
            P("energy", None),
            P("energy"),
            P(),
            P(),
            P("slab", None),
        ),
        out_specs=(P("energy", "slab", None, None, None), P("energy", "slab", None)),
        check_vma=False,
    )
```

time: 409 us -> 200 us (0.49)
  blocking collectives: 306 us -> 0 us
  Pallas kernels: 0 us -> 193 us
  starting transfers between devices: 48.8 us -> 0 us
  local copies, waits for them, and re-layouts: 30.2 us -> 5.24 us
  matrix products: 18.8 us -> 0 us
    all_gather x1 -> x0, blocking collectives: 306 us -> none  [on_device(): everyone = lax.all_gather(stacked_diag, 'energy', axis=0, tiled=True)]
    pallas_call x0 -> x1, Pallas kernels: none -> 193 us  [on_device(): pl.pallas_call(body, out_shape=(jax.ShapeDtypeStruct((2, NORB, NORB), BF1...]
    ppermute x4 -> x0, starting transfers between devices: 48.8 us -> none  [the longest x1 35.3 us: extended(): lax.ppermute(lax.slice_in_dim(block, 0, width, axis=dim), axis, backward)]
    dot_general x4 -> x0, matrix products: 18.8 us -> none  [the longest x1 9.97 us: on_device(): jnp.einsum('sij,escjk->escik', dipole, mixed, preferred_element_type=jnp....]
    gather x1 -> x0, local copies, waits for them, and re-layouts: 16.3 us -> none  [on_device(): jnp.diagonal(lesser[:, :, 1], axis1=-2, axis2=-1).astype(jnp.float32)]
    unnamed x15 -> x4, local copies, waits for them, and re-layouts: 9.44 us -> 5.24 us
  transfers between devices with their start and end apart: 4 -> 0, of which waited for: 0 -> 0; matrix products, arithmetic and copies ran while one was open for 5% -> 0% of each run, Pallas kernels for 0% -> 0%
where the time goes in v1:
time: 200 us
  Pallas kernels  193 us (96%)
  local copies, waits for them, and re-layouts  5.24 us (3%)
    pallas_call x1, Pallas kernels, on_device(): pl.pallas_call(body, out_shape=(jax.ShapeDtypeStruct((2, NORB, NORB), BF1...  193 us
    unnamed x4, local copies, waits for them, and re-layouts  5.24 us

profile of v1, /device:TPU:1, one launch (start us, length us, event | category | flops | bytes accessed | tf_op | source)
XLA Modules:
  0.0 199.8 jit_solution(7684877758798862738)
XLA Ops:
  1.3 193.3 %stencil.1 = (bf16[2,1024,1024]{2,1,0:T(8,128)(2,1)}, f32[8,128]{1,0:T(8,128)}) custom-call(bf16[2,1024,1024]{2,1,0:T(8,128)(2,1)} %bitcast.8, f32[8,128]{1,0:T(8,128)} %bitcast.10, bf16[1024,1024]{1,0:T(8,128)(2,1)} %bitcast.9, f32[1,3]{1,0:T(1,128)} %weights.1, s32[1]{0:T(128)S(6)} %copy.12.flags, s32[6]{0:T(128)} %lags.1, f32[2,6]{1,0:T(2,128)} %strengths.1, ...), custom_call_target="tpu_custom_call" | custom-call | flops 8589934592 | bytes 10485760 | tf_op jit(solution)/shard_map/stencil/pallas_call | solution.py:352
  194.6 0.0 copy-start
  194.6 4.6 %copy.13 = bf16[1,1,2,1024,1024]{4,3,2,1,0:T(8,128)(2,1)} copy(bf16[1,1,2,1024,1024]{4,3,2,1,0:T(8,128)(2,1)} %bitcast.6) | data formatting | bytes 8388608
  199.2 0.0 copy-done
  199.2 0.6 copy.14
Async XLA Ops:
  194.6 4.7 %copy-start = (f32[8,128]{1,0:T(8,128)S(1)}, f32[8,128]{1,0:T(8,128)}, u32[]{:S(2)}) copy-start(f32[8,128]{1,0:T(8,128)} %get-tuple-element.5) | copy-start | bytes 12292

commit v2 on v1

--- a/solution.py
+++ b/solution.py
@@ -16,7 +16,12 @@
 NORB = 1024
 ROWS = 128
 CHUNKS = NORB // ROWS
-LAG = 2
+TILE = 128
+PER = TILE // ROWS
+AHEAD = 3
+LAG_SUM = 1
+LAG_OWN = 3
+STAGES = (2, 3, 4)
 BLOCK = 256
 LANE = 128
 
@@ -26,9 +31,9 @@
 def body(
     lesser, great, dip, weights, flags, lags, strengths, coupling,
     out, great_out,
-    g_v, d_v, crossed, low, high, blow, bhigh, sums, sums_out, left, acc, stage,
-    zbuf, pbuf, qbuf, nbuf, nsend, phon, wsend, wrecv,
-    send, recv, zs, zr, ps, pr, ns, nr, ws, wr, local, osem,
+    g_v, d_v, d_t, crossed, low, high, blow, bhigh, sums, sums_out, left, acc,
+    diagonal, zbuf, pbuf, qbuf, nbuf, nsend, phon, wsend, wrecv,
+    send, recv, zs, zr, ps, pr, ns, nr, ws, wr, local,
 ):
     e = lax.axis_index("energy")
     s = lax.axis_index("slab")
@@ -83,13 +88,14 @@
     pl.semaphore_wait(barrier, expected)
 
     def chunk_copy(stream, k):
+        rows = pl.ds(pl.multiple_of(k * ROWS, ROWS), ROWS)
         source, target, device = {
-            CROSS: (lesser.at[0, pl.ds(k * ROWS, ROWS)], crossed.at[k], mirror),
-            LOW: (crossed.at[k], low.at[k], at(w - a_low)),
-            HIGH: (crossed.at[k], high.at[k], at(w - a_high)),
-            BLOW: (lesser.at[1, pl.ds(k * ROWS, ROWS)], blow.at[k], at(w - b_low)),
-            BHIGH: (lesser.at[1, pl.ds(k * ROWS, ROWS)], bhigh.at[k], at(w - b_high)),
-            SUMS: (sums_out.at[k], sums.at[k], mirror),
+            CROSS: (lesser.at[0, rows], crossed.at[rows], mirror),
+            LOW: (crossed.at[rows], low.at[rows], at(w - a_low)),
+            HIGH: (crossed.at[rows], high.at[rows], at(w - a_high)),
+            BLOW: (lesser.at[1, rows], blow.at[rows], at(w - b_low)),
+            BHIGH: (lesser.at[1, rows], bhigh.at[rows], at(w - b_high)),
+            SUMS: (sums_out.at[rows], sums.at[rows], mirror),
         }[stream]
         return pltpu.make_async_remote_copy(
             source, target, send.at[stream, k], recv.at[stream, k],
@@ -141,19 +147,19 @@
     )
     weight_copy.start()
 
-    @pl.loop(0, CHUNKS)
+    @pl.loop(0, AHEAD)
     def _(k):
+        start(CROSS, k)
         start(BHIGH, k)
         start(BLOW, k)
-        start(CROSS, k)
 
     for stream, buffer in ((LOW, low), (HIGH, high), (BLOW, blow), (BHIGH, bhigh)):
 
         @pl.when(jnp.logical_not(hears[stream]))
         def _():
-            @pl.loop(0, CHUNKS)
+            @pl.loop(0, NORB // TILE)
             def _(k):
-                buffer[k] = jnp.zeros((ROWS, NORB), BF16)
+                buffer[pl.ds(pl.multiple_of(k * TILE, TILE), TILE)] = jnp.zeros((TILE, NORB), BF16)
 
     eye = lax.broadcasted_iota(jnp.int32, (LANE, LANE), 0) == lax.broadcasted_iota(
         jnp.int32, (LANE, LANE), 1
@@ -162,8 +168,9 @@
     for b in range(NORB // LANE):
         part = slice(b * LANE, (b + 1) * LANE)
         tile = jnp.where(eye, g_v[1, part, part].astype(F32), 0.0)
-        zbuf[0, b : b + 1, :] = jnp.sum(tile, axis=0, keepdims=True)
-    zbuf[0, 8:16, :] = great[...]
+        diagonal[b : b + 1, :] = jnp.sum(tile, axis=0, keepdims=True)
+    diagonal[8:16, :] = great[...]
+    zbuf[0] = diagonal[...].astype(BF16)
 
     def ring_copy(d):
         return pltpu.make_async_remote_copy(
@@ -182,6 +189,12 @@
 
     copies_in[1].wait()
     copies_in[2].wait()
+
+    @pl.loop(0, NORB // LANE)
+    def _(i):
+        part = pl.ds(pl.multiple_of(i * LANE, LANE), LANE)
+        d_t[:, part] = d_v[part, :].T
+
     weight_copy.wait()
     m_low, m_high = wrecv[0, 0:1, 0:1], wrecv[1, 0:1, 0:1]
 
@@ -210,8 +223,9 @@
                     first, second = strengths[0, m], strengths[1, m]
                     k_less += jnp.where(up, first, 0.0) + jnp.where(down, second, 0.0)
                     k_great += jnp.where(up, second, 0.0) + jnp.where(down, first, 0.0)
-                less += k_less * zbuf[d, 0:8, :]
-                more += k_great * zbuf[d, 8:16, :]
+                held = diagonal[...] if d == 0 else zbuf[d].astype(F32)
+                less += k_less * held[0:8]
+                more += k_great * held[8:16]
             pbuf[t, 0:8, :] = less
             pbuf[t, 8:16, :] = more
 
@@ -266,105 +280,145 @@
             phon[part, :] = nsend[1, part, :] + nbuf[0, part, :] + coupling[...] * nbuf[1, part, :]
         great_out[...] = phon[8:16, :]
 
-    def multiply(c, k, mixed):
-        left[c] = lax.dot_general(
-            mixed, d_v[...], (((1,), (1,)), ((), ())), preferred_element_type=F32
-        ).astype(BF16)
-        columns = pl.ds(pl.multiple_of(k * ROWS, ROWS), ROWS)
+    def multiply(c, tile, mixed, last):
+        left[c] = jnp.dot(mixed, d_t[...], preferred_element_type=F32).astype(BF16)
+        if not last:
+
+            @pl.loop(0, NORB // BLOCK)
+            def _(i):
+                rows = pl.ds(pl.multiple_of(i * BLOCK, BLOCK), BLOCK)
+                acc[c, rows, :] += jnp.dot(d_v[rows, tile], left[c], preferred_element_type=F32)
+
+            return
 
         @pl.loop(0, NORB // BLOCK)
         def _(i):
             rows = pl.ds(pl.multiple_of(i * BLOCK, BLOCK), BLOCK)
-            acc[c, rows, :] += jnp.dot(d_v[rows, columns], left[c], preferred_element_type=F32)
-
-    def own(c, k):
-        return own_w * g_v[c, pl.ds(k * ROWS, ROWS), :].astype(F32)
-
-    @pl.loop(0, CHUNKS + LAG)
-    def _(k):
-        @pl.when(k < CHUNKS)
-        def _():
-            arrive(CROSS, k)
-            start(LOW, k)
-            start(HIGH, k)
-            arrive(BLOW, k)
-            arrive(BHIGH, k)
-            sums_out[k] = (m_low * blow[k].astype(F32) + m_high * bhigh[k].astype(F32)).astype(BF16)
-            start(SUMS, k)
-
-        @pl.when(k == 2)
-        def _():
-            partial_sums()
-
-        @pl.when(k == 4)
-        def _():
-            correlate()
-
-        @pl.when(k == 6)
-        def _():
-            couple()
-
-        @pl.when(k >= LAG)
-        def _():
-            j = k - LAG
-            arrive(SUMS, j)
-            multiply(1, j, (own(1, j) + sums[j].astype(F32)).astype(BF16))
-
-    def write(c):
-        return pltpu.make_async_copy(stage.at[c], out.at[c], osem.at[c])
-
-    def finish(c):
-        for i in range(NORB // LANE):
-            rows = slice(i * LANE, (i + 1) * LANE)
-            stage[c, rows, :] = acc[c, rows, :].astype(BF16)
+            total = acc[c, rows, :] + jnp.dot(
+                d_v[rows, tile], left[c], preferred_element_type=F32
+            )
             if c == 1:
-                stage[1, rows, rows] = (
+                acc[1, rows, :] = total
+            out[c, rows, :] = total.astype(BF16)
+
+        if c == 1:
+            for i in range(NORB // LANE):
+                rows = slice(i * LANE, (i + 1) * LANE)
+                out[1, rows, rows] = (
                     acc[1, rows, rows] + jnp.where(eye, phon[i : i + 1, :], 0.0)
                 ).astype(BF16)
-        write(c).start()
-
-    finish(1)
+
+    def with_sums(group, last=False):
+        for i in range(PER):
+            arrive(SUMS, group * PER + i)
+        tile = pl.ds(pl.multiple_of(group * TILE, TILE), TILE)
+        mixed = own_w * g_v[1, tile].astype(F32) + sums[tile].astype(F32)
+        multiply(1, tile, mixed.astype(BF16), last)
+
+    def with_sides(group, last=False):
+        for i in range(PER):
+            arrive(LOW, group * PER + i)
+            arrive(HIGH, group * PER + i)
+        tile = pl.ds(pl.multiple_of(group * TILE, TILE), TILE)
+        mixed = (
+            own_w * g_v[0, tile].astype(F32)
+            + low_w * low[tile].astype(F32)
+            + high_w * high[tile].astype(F32)
+        )
+        multiply(0, tile, mixed.astype(BF16), last)
 
     @pl.loop(0, CHUNKS)
     def _(k):
-        arrive(LOW, k)
-        arrive(HIGH, k)
-        mixed = own(0, k) + low_w * low[k].astype(F32) + high_w * high[k].astype(F32)
-        multiply(0, k, mixed.astype(BF16))
-
-    finish(0)
+        arrive(CROSS, k)
+        start(HIGH, k)
+        start(LOW, k)
+
+        @pl.when(k + AHEAD < CHUNKS)
+        def _():
+            start(CROSS, k + AHEAD)
+
+        arrive(BLOW, k)
+        arrive(BHIGH, k)
+
+        @pl.when(k + AHEAD < CHUNKS)
+        def _():
+            start(BHIGH, k + AHEAD)
+            start(BLOW, k + AHEAD)
+
+        rows = pl.ds(pl.multiple_of(k * ROWS, ROWS), ROWS)
+        sums_out[rows] = (
+            m_low * blow[rows].astype(F32) + m_high * bhigh[rows].astype(F32)
+        ).astype(BF16)
+        start(SUMS, k)
+
+        for stage_at, action in zip(STAGES, (partial_sums, correlate, couple)):
+
+            @pl.when(k == stage_at)
+            def _():
+                action()
+
+        j = k - LAG_SUM
+
+        @pl.when(jnp.logical_and(j >= 0, j % PER == PER - 1))
+        def _():
+            with_sums(j // PER)
+
+        i = k - LAG_OWN
+
+        @pl.when(jnp.logical_and(i >= 0, i % PER == PER - 1))
+        def _():
+            with_sides(i // PER)
+
+    groups = CHUNKS // PER
+    for group in range((CHUNKS - LAG_SUM) // PER, groups):
+        with_sums(group, group == groups - 1)
+    for group in range((CHUNKS - LAG_OWN) // PER, groups):
+        with_sides(group, group == groups - 1)
 
     @pl.loop(0, CHUNKS)
     def _(k):
         for stream in (CROSS, LOW, HIGH, BLOW, BHIGH, SUMS):
             sent(stream, k)
 
-    write(1).wait()
-    write(0).wait()
+
+def store(result, great_result, out, great_out, sems):
+    copies = [
+        pltpu.make_async_copy(result, out, sems.at[0]),
+        pltpu.make_async_copy(great_result, great_out, sems.at[1]),
+    ]
+    for copy in copies:
+        copy.start()
+    for copy in copies:
+        copy.wait()
+
+
+def in_hbm(x):
+    return pltpu.with_memory_space_constraint(x, pltpu.HBM)
 
 
 def on_device(lesser, great, dipole, weights, flags, lags, strengths, coupling):
     vmem = pl.BlockSpec(memory_space=pltpu.VMEM)
     smem = pl.BlockSpec(memory_space=pltpu.SMEM)
-    hbm = pl.BlockSpec(memory_space=pl.ANY)
-    chunks = pltpu.VMEM((CHUNKS, ROWS, NORB), BF16)
+    hbm = pl.BlockSpec(memory_space=pltpu.HBM)
+    chunks = pltpu.VMEM((NORB, NORB), BF16)
     dma = pltpu.SemaphoreType.DMA
-    out, great_out = pl.pallas_call(
+    result, great_result = pl.pallas_call(
         body,
         out_shape=(
-            jax.ShapeDtypeStruct((2, NORB, NORB), BF16),
-            jax.ShapeDtypeStruct((8, LANE), F32),
+            pltpu.VMEM((2, NORB, NORB), BF16),
+            pltpu.VMEM((8, LANE), F32),
         ),
         in_specs=[hbm, vmem, hbm, smem, smem, smem, smem, vmem],
-        out_specs=(hbm, vmem),
+        out_specs=(vmem, vmem),
         scratch_shapes=[
             pltpu.VMEM((2, NORB, NORB), BF16),
             pltpu.VMEM((NORB, NORB), BF16),
+            pltpu.VMEM((NORB, NORB), BF16),
             chunks, chunks, chunks, chunks, chunks, chunks, chunks,
-            pltpu.VMEM((2, ROWS, NORB), BF16),
+            pltpu.VMEM((2, TILE, NORB), BF16),
             pltpu.VMEM((2, NORB, NORB), F32),
-            pltpu.VMEM((2, NORB, NORB), BF16),
-            pltpu.VMEM((RING, 16, LANE), F32),
+            pltpu.VMEM((16, LANE), F32),
+            pltpu.VMEM((RING, 16, LANE), BF16),
             pltpu.VMEM((RING, 16, LANE), F32),
             pltpu.VMEM((RING, 16, LANE), F32),
             pltpu.VMEM((2, 16, LANE), F32),
@@ -377,19 +431,32 @@
             dma((RING,)), dma((RING,)),
             dma((2,)), dma((2,)),
             dma, dma,
-            dma((3,)), dma((2,)),
+            dma((3,)),
         ],
         name="stencil",
         cost_estimate=pl.CostEstimate(
             flops=8 * NORB**3, bytes_accessed=10 * NORB * NORB, transcendentals=0
         ),
         compiler_params=pltpu.CompilerParams(
-            collective_id=0, has_side_effects=True, vmem_limit_bytes=56 << 20
+            collective_id=0, has_side_effects=True, vmem_limit_bytes=40 << 20
         ),
     )(
-        lesser.reshape(2, NORB, NORB), great.reshape(8, LANE), dipole.reshape(NORB, NORB),
-        weights, flags, lags, strengths, coupling.reshape(8, LANE),
+        in_hbm(lesser.reshape(2, NORB, NORB)), in_hbm(great.reshape(8, LANE)),
+        in_hbm(dipole.reshape(NORB, NORB)), in_hbm(weights), flags, in_hbm(lags),
+        in_hbm(strengths), in_hbm(coupling.reshape(8, LANE)),
     )
+    out, great_out = pl.pallas_call(
+        store,
+        out_shape=(
+            jax.ShapeDtypeStruct((2, NORB, NORB), BF16),
+            jax.ShapeDtypeStruct((8, LANE), F32),
+        ),
+        in_specs=[vmem, vmem],
+        out_specs=(hbm, hbm),
+        scratch_shapes=[dma((2,))],
+        name="store",
+        compiler_params=pltpu.CompilerParams(vmem_limit_bytes=8 << 20),
+    )(result, great_result)
     return out.reshape(1, 1, 2, NORB, NORB), great_out.reshape(1, 1, NORB)
 
 

time: 200 us -> 155 us (0.78)
  the two profiles are of different devices: /device:TPU:1 before, /device:TPU:40 now
where the time goes in v2:
time: 155 us
  Pallas kernels  153 us (99%)
    pallas_call x1, Pallas kernels, on_device(): pl.pallas_call(body, out_shape=(pltpu.VMEM((2, NORB, NORB), BF16), pltpu....  151 us

profile of v2, /device:TPU:40, one launch (start us, length us, event | category | flops | bytes accessed | tf_op | source)
XLA Modules:
  0.0 154.6 jit_solution(14981205999701113480)
XLA Ops:
  1.3 151.2 %stencil.1 = (bf16[2,1024,1024]{2,1,0:T(8,128)(2,1)S(1)}, f32[8,128]{1,0:T(8,128)S(1)}) custom-call(bf16[2,1024,1024]{2,1,0:T(8,128)(2,1)} %bitcast.6, f32[8,128]{1,0:T(8,128)} %bitcast.9, bf16[1024,1024]{1,0:T(8,128)(2,1)} %bitcast.8, f32[1,3]{1,0:T(1,128)} %weights.1, s32[1]{0:T(128)S(6)} %copy.10.flags, s32[6]{0:T(128)} %lags.1, f32[2,6]{1,0:T(2,128)} %strengths.1, ...), custom_call_target="tpu_custom_call" | custom-call | flops 8589934592 | bytes 10485760 | tf_op jit(solution)/shard_map/stencil/pallas_call | solution.py:405
  152.5 2.0 %store.1 = (bf16[2,1024,1024]{2,1,0:T(8,128)(2,1)}, f32[8,128]{1,0:T(8,128)}) custom-call(bf16[2,1024,1024]{2,1,0:T(8,128)(2,1)S(1)} %get-tuple-element.6.result, f32[8,128]{1,0:T(8,128)S(1)} %get-tuple-element.7.great_result), custom_call_target="tpu_custom_call" | custom-call | tf_op jit(solution)/shard_map/store/pallas_call | solution.py:448

commit v3 on v2

--- a/solution.py
+++ b/solution.py
@@ -18,10 +18,10 @@
 CHUNKS = NORB // ROWS
 TILE = 128
 PER = TILE // ROWS
-AHEAD = 3
+AHEAD = 4
 LAG_SUM = 1
-LAG_OWN = 3
-STAGES = (2, 3, 4)
+LAG_OWN = 4
+STAGES = (3, 4, 5)
 BLOCK = 256
 LANE = 128
 
@@ -29,9 +29,9 @@
 
 
 def body(
-    lesser, great, dip, weights, flags, lags, strengths, coupling,
-    out, great_out,
-    g_v, d_v, d_t, crossed, low, high, blow, bhigh, sums, sums_out, left, acc,
+    lesser, great_in, dip, weights_in, flags, lags_in, strengths_in, coupling_in,
+    total_real, left_last, d_last, out_imag, great_out,
+    great, coupling, weights, lags, strengths, g_v, d_v, d_t, crossed, low, high, blow, bhigh, sums, sums_out, left, total_imag,
     diagonal, zbuf, pbuf, qbuf, nbuf, nsend, phon, wsend, wrecv,
     send, recv, zs, zr, ps, pr, ns, nr, ws, wr, local,
 ):
@@ -50,13 +50,12 @@
     a_low, a_high = h - 2, h + 1
     b_low, b_high = -1 - h, 2 - h
 
-    copies_in = [
-        pltpu.make_async_copy(lesser.at[1], g_v.at[1], local.at[0]),
-        pltpu.make_async_copy(lesser.at[0], g_v.at[0], local.at[1]),
-        pltpu.make_async_copy(dip, d_v, local.at[2]),
-    ]
-    for copy in copies_in:
-        copy.start()
+    pairs = (
+        (weights_in, weights), (great_in, great), (lesser.at[1], g_v.at[1]),
+        (lags_in, lags), (strengths_in, strengths), (coupling_in, coupling),
+        (lesser.at[0], g_v.at[0]), (dip, d_v),
+    )
+    copies_in = [pltpu.make_async_copy(*pair, local.at[i]) for i, pair in enumerate(pairs)]
 
     barrier = pltpu.get_barrier_semaphore()
     expected = jnp.int32(2 * (RING - 1))
@@ -138,6 +137,17 @@
         else:
             chunk_copy(stream, k).wait_send()
 
+    @pl.loop(0, AHEAD)
+    def _(k):
+        start(CROSS, k)
+        start(BHIGH, k)
+        start(BLOW, k)
+
+    for copy in copies_in:
+        copy.start()
+    for copy in copies_in[:3]:
+        copy.wait()
+
     flag = flags[0].astype(F32)
     own_w, low_w, high_w = weights[0, 0], flag * weights[0, 1], flag * weights[0, 2]
     wsend[0] = jnp.full((8, LANE), low_w, F32)
@@ -147,12 +157,6 @@
     )
     weight_copy.start()
 
-    @pl.loop(0, AHEAD)
-    def _(k):
-        start(CROSS, k)
-        start(BHIGH, k)
-        start(BLOW, k)
-
     for stream, buffer in ((LOW, low), (HIGH, high), (BLOW, blow), (BHIGH, bhigh)):
 
         @pl.when(jnp.logical_not(hears[stream]))
@@ -164,7 +168,6 @@
     eye = lax.broadcasted_iota(jnp.int32, (LANE, LANE), 0) == lax.broadcasted_iota(
         jnp.int32, (LANE, LANE), 1
     )
-    copies_in[0].wait()
     for b in range(NORB // LANE):
         part = slice(b * LANE, (b + 1) * LANE)
         tile = jnp.where(eye, g_v[1, part, part].astype(F32), 0.0)
@@ -181,19 +184,22 @@
     for d in range(1, RING):
         ring_copy(d).start()
 
-    for c in range(2):
+    totals = (total_real, total_imag)
+    for total in totals:
 
         @pl.loop(0, NORB // BLOCK)
         def _(i):
-            acc[c, pl.ds(i * BLOCK, BLOCK), :] = jnp.zeros((BLOCK, NORB), F32)
-
-    copies_in[1].wait()
-    copies_in[2].wait()
+            total[pl.ds(i * BLOCK, BLOCK), :] = jnp.zeros((BLOCK, NORB), F32)
+
+    for copy in copies_in[3:]:
+        copy.wait()
 
     @pl.loop(0, NORB // LANE)
     def _(i):
         part = pl.ds(pl.multiple_of(i * LANE, LANE), LANE)
         d_t[:, part] = d_v[part, :].T
+
+    d_last[...] = d_v[:, NORB - TILE :]
 
     weight_copy.wait()
     m_low, m_high = wrecv[0, 0:1, 0:1], wrecv[1, 0:1, 0:1]
@@ -281,31 +287,27 @@
         great_out[...] = phon[8:16, :]
 
     def multiply(c, tile, mixed, last):
-        left[c] = jnp.dot(mixed, d_t[...], preferred_element_type=F32).astype(BF16)
-        if not last:
-
-            @pl.loop(0, NORB // BLOCK)
-            def _(i):
-                rows = pl.ds(pl.multiple_of(i * BLOCK, BLOCK), BLOCK)
-                acc[c, rows, :] += jnp.dot(d_v[rows, tile], left[c], preferred_element_type=F32)
-
+        product = jnp.dot(mixed, d_t[...], preferred_element_type=F32).astype(BF16)
+        if last and c == 0:
+            left_last[...] = product
             return
+        left[c] = product
 
         @pl.loop(0, NORB // BLOCK)
         def _(i):
             rows = pl.ds(pl.multiple_of(i * BLOCK, BLOCK), BLOCK)
-            total = acc[c, rows, :] + jnp.dot(
+            total = totals[c][rows, :] + jnp.dot(
                 d_v[rows, tile], left[c], preferred_element_type=F32
             )
-            if c == 1:
-                acc[1, rows, :] = total
-            out[c, rows, :] = total.astype(BF16)
-
-        if c == 1:
+            totals[c][rows, :] = total
+            if last:
+                out_imag[rows, :] = total.astype(BF16)
+
+        if last:
             for i in range(NORB // LANE):
                 rows = slice(i * LANE, (i + 1) * LANE)
-                out[1, rows, rows] = (
-                    acc[1, rows, rows] + jnp.where(eye, phon[i : i + 1, :], 0.0)
+                out_imag[rows, rows] = (
+                    total_imag[rows, rows] + jnp.where(eye, phon[i : i + 1, :], 0.0)
                 ).astype(BF16)
 
     def with_sums(group, last=False):
@@ -372,22 +374,39 @@
     groups = CHUNKS // PER
     for group in range((CHUNKS - LAG_SUM) // PER, groups):
         with_sums(group, group == groups - 1)
-    for group in range((CHUNKS - LAG_OWN) // PER, groups):
-        with_sides(group, group == groups - 1)
+    for group in range((CHUNKS - LAG_OWN) // PER, groups - 1):
+        with_sides(group)
 
     @pl.loop(0, CHUNKS)
     def _(k):
-        for stream in (CROSS, LOW, HIGH, BLOW, BHIGH, SUMS):
+        for stream in (CROSS, BLOW, BHIGH, SUMS):
             sent(stream, k)
 
-
-def store(result, great_result, out, great_out, sems):
-    copies = [
-        pltpu.make_async_copy(result, out, sems.at[0]),
-        pltpu.make_async_copy(great_result, great_out, sems.at[1]),
-    ]
+    @pl.loop(0, CHUNKS - PER)
+    def _(k):
+        for stream in (LOW, HIGH):
+            sent(stream, k)
+
+    with_sides(groups - 1, True)
+    for k in range(CHUNKS - PER, CHUNKS):
+        for stream in (LOW, HIGH):
+            sent(stream, k)
+
+
+def store(total, left, dip, imag, great, out, great_out, stage, sems):
+    copies = [pltpu.make_async_copy(great, great_out, sems.at[2, 0])]
+    blocks = [slice(i * BLOCK, (i + 1) * BLOCK) for i in range(NORB // BLOCK)]
+    for i, rows in enumerate(blocks):
+        copies.append(pltpu.make_async_copy(imag.at[rows], out.at[1, rows], sems.at[1, i]))
     for copy in copies:
         copy.start()
+    for i, rows in enumerate(blocks):
+        stage[rows, :] = (
+            total[rows, :] + jnp.dot(dip[rows, :], left[...], preferred_element_type=F32)
+        ).astype(BF16)
+        copy = pltpu.make_async_copy(stage.at[rows], out.at[0, rows], sems.at[0, i])
+        copy.start()
+        copies.append(copy)
     for copy in copies:
         copy.wait()
 
@@ -398,25 +417,30 @@
 
 def on_device(lesser, great, dipole, weights, flags, lags, strengths, coupling):
     vmem = pl.BlockSpec(memory_space=pltpu.VMEM)
-    smem = pl.BlockSpec(memory_space=pltpu.SMEM)
+    smem = pltpu.SMEM
     hbm = pl.BlockSpec(memory_space=pltpu.HBM)
     chunks = pltpu.VMEM((NORB, NORB), BF16)
     dma = pltpu.SemaphoreType.DMA
-    result, great_result = pl.pallas_call(
+    results = pl.pallas_call(
         body,
         out_shape=(
-            pltpu.VMEM((2, NORB, NORB), BF16),
+            pltpu.VMEM((NORB, NORB), F32),
+            pltpu.VMEM((TILE, NORB), BF16),
+            pltpu.VMEM((NORB, TILE), BF16),
+            pltpu.VMEM((NORB, NORB), BF16),
             pltpu.VMEM((8, LANE), F32),
         ),
-        in_specs=[hbm, vmem, hbm, smem, smem, smem, smem, vmem],
-        out_specs=(vmem, vmem),
+        in_specs=[hbm] * 4 + [pl.BlockSpec(memory_space=smem)] + [hbm] * 3,
+        out_specs=(vmem,) * 5,
         scratch_shapes=[
+            pltpu.VMEM((8, LANE), F32), pltpu.VMEM((8, LANE), F32),
+            smem((1, 3), F32), smem((MODES,), jnp.int32), smem((2, MODES), F32),
             pltpu.VMEM((2, NORB, NORB), BF16),
             pltpu.VMEM((NORB, NORB), BF16),
             pltpu.VMEM((NORB, NORB), BF16),
             chunks, chunks, chunks, chunks, chunks, chunks, chunks,
             pltpu.VMEM((2, TILE, NORB), BF16),
-            pltpu.VMEM((2, NORB, NORB), F32),
+            pltpu.VMEM((NORB, NORB), F32),
             pltpu.VMEM((16, LANE), F32),
             pltpu.VMEM((RING, 16, LANE), BF16),
             pltpu.VMEM((RING, 16, LANE), F32),
@@ -431,7 +455,7 @@
             dma((RING,)), dma((RING,)),
             dma((2,)), dma((2,)),
             dma, dma,
-            dma((3,)),
+            dma((8,)),
         ],
         name="stencil",
         cost_estimate=pl.CostEstimate(
@@ -451,12 +475,12 @@
             jax.ShapeDtypeStruct((2, NORB, NORB), BF16),
             jax.ShapeDtypeStruct((8, LANE), F32),
         ),
-        in_specs=[vmem, vmem],
+        in_specs=[vmem] * 5,
         out_specs=(hbm, hbm),
-        scratch_shapes=[dma((2,))],
+        scratch_shapes=[pltpu.VMEM((NORB, NORB), BF16), dma((3, NORB // BLOCK))],
         name="store",
         compiler_params=pltpu.CompilerParams(vmem_limit_bytes=8 << 20),
-    )(result, great_result)
+    )(*results)
     return out.reshape(1, 1, 2, NORB, NORB), great_out.reshape(1, 1, NORB)
 
 

time: 155 us -> 153 us (0.987)
  Pallas kernels: 153 us -> 151 us
    pallas_call x1, Pallas kernels: 151 us -> 149 us  [on_device(): pl.pallas_call(body, out_shape=(pltpu.VMEM((NORB, NORB), F32), pltpu.VMEM...]
where the time goes in v3:
time: 153 us
  Pallas kernels  151 us (99%)
    pallas_call x1, Pallas kernels, on_device(): pl.pallas_call(body, out_shape=(pltpu.VMEM((NORB, NORB), F32), pltpu.VMEM...  149 us

profile of v3, /device:TPU:40, one launch (start us, length us, event | category | flops | bytes accessed | tf_op | source)
XLA Modules:
  0.0 152.7 jit_solution(14418227680516340947)
XLA Ops:
  1.3 149.3 %stencil.1 = (f32[1024,1024]{1,0:T(8,128)S(1)}, bf16[128,1024]{1,0:T(8,128)(2,1)S(1)}, bf16[1024,128]{1,0:T(8,128)(2,1)S(1)}, bf16[1024,1024]{1,0:T(8,128)(2,1)S(1)}, f32[8,128]{1,0:T(8,128)S(1)}) custom-call(bf16[2,1024,1024]{2,1,0:T(8,128)(2,1)} %bitcast.6, f32[8,128]{1,0:T(8,128)} %bitcast.9, bf16[1024,1024]{1,0:T(8,128)(2,1)} %bitcast.8, ...), custom_call_target="tpu_custom_call" | custom-call | flops 8589934592 | bytes 10485760 | tf_op jit(solution)/shard_map/stencil/pallas_call | solution.py:424
  150.6 2.1 %store.1 = (bf16[2,1024,1024]{2,1,0:T(8,128)(2,1)}, f32[8,128]{1,0:T(8,128)}) custom-call(f32[1024,1024]{1,0:T(8,128)S(1)} %get-tuple-element.9.total, bf16[128,1024]{1,0:T(8,128)(2,1)S(1)} %get-tuple-element.10.left, bf16[1024,128]{1,0:T(8,128)(2,1)S(1)} %get-tuple-element.11.dip, bf16[1024,1024]{1,0:T(8,128)(2,1)S(1)} %get-tuple-element.12.imag, ...), custom_call_target="tpu_custom_call" | custom-call | tf_op jit(solution)/shard_map/store/pallas_call | solution.py:472

commit v4 on v3

--- a/solution.py
+++ b/solution.py
@@ -18,9 +18,9 @@
 CHUNKS = NORB // ROWS
 TILE = 128
 PER = TILE // ROWS
-AHEAD = 4
+AHEAD = 5
 LAG_SUM = 1
-LAG_OWN = 4
+LAG_OWN = 6
 STAGES = (3, 4, 5)
 BLOCK = 256
 LANE = 128
@@ -30,8 +30,8 @@
 
 def body(
     lesser, great_in, dip, weights_in, flags, lags_in, strengths_in, coupling_in,
-    total_real, left_last, d_last, out_imag, great_out,
-    great, coupling, weights, lags, strengths, g_v, d_v, d_t, crossed, low, high, blow, bhigh, sums, sums_out, left, total_imag,
+    total_real, mixed_last, d_t, d_last, out_imag, great_out,
+    great, coupling, weights, lags, strengths, g_v, d_v, crossed, low, high, blow, bhigh, sums, sums_out, left, total_imag,
     diagonal, zbuf, pbuf, qbuf, nbuf, nsend, phon, wsend, wrecv,
     send, recv, zs, zr, ps, pr, ns, nr, ws, wr, local,
 ):
@@ -287,11 +287,10 @@
         great_out[...] = phon[8:16, :]
 
     def multiply(c, tile, mixed, last):
-        product = jnp.dot(mixed, d_t[...], preferred_element_type=F32).astype(BF16)
         if last and c == 0:
-            left_last[...] = product
+            mixed_last[...] = mixed
             return
-        left[c] = product
+        left[c] = jnp.dot(mixed, d_t[...], preferred_element_type=F32).astype(BF16)
 
         @pl.loop(0, NORB // BLOCK)
         def _(i):
@@ -393,13 +392,14 @@
             sent(stream, k)
 
 
-def store(total, left, dip, imag, great, out, great_out, stage, sems):
+def store(total, mixed, d_t, dip, imag, great, out, great_out, left, stage, sems):
     copies = [pltpu.make_async_copy(great, great_out, sems.at[2, 0])]
     blocks = [slice(i * BLOCK, (i + 1) * BLOCK) for i in range(NORB // BLOCK)]
     for i, rows in enumerate(blocks):
         copies.append(pltpu.make_async_copy(imag.at[rows], out.at[1, rows], sems.at[1, i]))
     for copy in copies:
         copy.start()
+    left[...] = jnp.dot(mixed[...], d_t[...], preferred_element_type=F32).astype(BF16)
     for i, rows in enumerate(blocks):
         stage[rows, :] = (
             total[rows, :] + jnp.dot(dip[rows, :], left[...], preferred_element_type=F32)
@@ -426,17 +426,17 @@
         out_shape=(
             pltpu.VMEM((NORB, NORB), F32),
             pltpu.VMEM((TILE, NORB), BF16),
+            pltpu.VMEM((NORB, NORB), BF16),
             pltpu.VMEM((NORB, TILE), BF16),
             pltpu.VMEM((NORB, NORB), BF16),
             pltpu.VMEM((8, LANE), F32),
         ),
         in_specs=[hbm] * 4 + [pl.BlockSpec(memory_space=smem)] + [hbm] * 3,
-        out_specs=(vmem,) * 5,
+        out_specs=(vmem,) * 6,
         scratch_shapes=[
             pltpu.VMEM((8, LANE), F32), pltpu.VMEM((8, LANE), F32),
             smem((1, 3), F32), smem((MODES,), jnp.int32), smem((2, MODES), F32),
             pltpu.VMEM((2, NORB, NORB), BF16),
-            pltpu.VMEM((NORB, NORB), BF16),
             pltpu.VMEM((NORB, NORB), BF16),
             chunks, chunks, chunks, chunks, chunks, chunks, chunks,
             pltpu.VMEM((2, TILE, NORB), BF16),
@@ -475,9 +475,13 @@
             jax.ShapeDtypeStruct((2, NORB, NORB), BF16),
             jax.ShapeDtypeStruct((8, LANE), F32),
         ),
-        in_specs=[vmem] * 5,
+        in_specs=[vmem] * 6,
         out_specs=(hbm, hbm),
-        scratch_shapes=[pltpu.VMEM((NORB, NORB), BF16), dma((3, NORB // BLOCK))],
+        scratch_shapes=[
+            pltpu.VMEM((TILE, NORB), BF16),
+            pltpu.VMEM((NORB, NORB), BF16),
+            dma((3, NORB // BLOCK)),
+        ],
         name="store",
         compiler_params=pltpu.CompilerParams(vmem_limit_bytes=8 << 20),
     )(*results)

time: 153 us -> 152 us (level)
  no operation moved by 1% of the time
where the time goes in v4:
time: 152 us
  Pallas kernels  151 us (99%)
    pallas_call x1, Pallas kernels, on_device(): pl.pallas_call(body, out_shape=(pltpu.VMEM((NORB, NORB), F32), pltpu.VMEM...  149 us

profile of v4, /device:TPU:40, one launch (start us, length us, event | category | flops | bytes accessed | tf_op | source)
XLA Modules:
  0.0 152.3 jit_solution(16404218570572924055)
XLA Ops:
  1.3 148.9 %stencil.1 = (f32[1024,1024]{1,0:T(8,128)S(1)}, bf16[128,1024]{1,0:T(8,128)(2,1)S(1)}, bf16[1024,1024]{1,0:T(8,128)(2,1)S(1)}, bf16[1024,128]{1,0:T(8,128)(2,1)S...) custom-call(bf16[2,1024,1024]{2,1,0:T(8,128)(2,1)} %bitcast.6, f32[8,128]{1,0:T(8,128)} %bitcast.9, ...), custom_call_target="tpu_custom_call" | custom-call | flops 8589934592 | bytes 10485760 | tf_op jit(solution)/shard_map/stencil/pallas_call | solution.py:424
  150.2 2.1 %store.1 = (bf16[2,1024,1024]{2,1,0:T(8,128)(2,1)}, f32[8,128]{1,0:T(8,128)}) custom-call(f32[1024,1024]{1,0:T(8,128)S(1)} %get-tuple-element.10.total, bf16[128,1024]{1,0:T(8,128)(2,1)S(1)} %get-tuple-element.11.mixed, bf16[1024,1024]{1,0:T(8,128)(2,1)S(1)} %get-tuple-element.12.d_t, bf16[1024,128]{1,0:T(8,128)(2,1)S(1)} %get-tuple-element.13.dip, ...), custom_call_target="tpu_custom_call" | custom-call | tf_op jit(solution)/shard_map/store/pallas_call | solution.py:472

commit v5 on v4

--- a/solution.py
+++ b/solution.py
@@ -19,6 +19,7 @@
 TILE = 128
 PER = TILE // ROWS
 AHEAD = 5
+AHEAD_CROSS = 2
 LAG_SUM = 1
 LAG_OWN = 6
 STAGES = (3, 4, 5)
@@ -137,9 +138,12 @@
         else:
             chunk_copy(stream, k).wait_send()
 
+    @pl.loop(0, AHEAD_CROSS)
+    def _(k):
+        start(CROSS, k)
+
     @pl.loop(0, AHEAD)
     def _(k):
-        start(CROSS, k)
         start(BHIGH, k)
         start(BLOW, k)
 
@@ -334,9 +338,9 @@
         start(HIGH, k)
         start(LOW, k)
 
-        @pl.when(k + AHEAD < CHUNKS)
-        def _():
-            start(CROSS, k + AHEAD)
+        @pl.when(k + AHEAD_CROSS < CHUNKS)
+        def _():
+            start(CROSS, k + AHEAD_CROSS)
 
         arrive(BLOW, k)
         arrive(BHIGH, k)

time: 152 us -> 154 us (1.013); the launches traced: 152 us -> 152 us
  no operation moved by 1% of the time
where the time goes in v5:
time: 154 us; the launch traced here: 152 us
  Pallas kernels  151 us (98%)
    pallas_call x1, Pallas kernels, on_device(): pl.pallas_call(body, out_shape=(pltpu.VMEM((NORB, NORB), F32), pltpu.VMEM...  149 us

profile of v5, /device:TPU:40, one launch (start us, length us, event | category | flops | bytes accessed | tf_op | source)
XLA Modules:
  0.0 152.3 jit_solution(16645389316674845893)
XLA Ops:
  1.3 148.9 %stencil.1 = (f32[1024,1024]{1,0:T(8,128)S(1)}, bf16[128,1024]{1,0:T(8,128)(2,1)S(1)}, bf16[1024,1024]{1,0:T(8,128)(2,1)S(1)}, bf16[1024,128]{1,0:T(8,128)(2,1)S...) custom-call(bf16[2,1024,1024]{2,1,0:T(8,128)(2,1)} %bitcast.6, f32[8,128]{1,0:T(8,128)} %bitcast.9, ...), custom_call_target="tpu_custom_call" | custom-call | flops 8589934592 | bytes 10485760 | tf_op jit(solution)/shard_map/stencil/pallas_call | solution.py:428
  150.2 2.1 %store.1 = (bf16[2,1024,1024]{2,1,0:T(8,128)(2,1)}, f32[8,128]{1,0:T(8,128)}) custom-call(f32[1024,1024]{1,0:T(8,128)S(1)} %get-tuple-element.10.total, bf16[128,1024]{1,0:T(8,128)(2,1)S(1)} %get-tuple-element.11.mixed, bf16[1024,1024]{1,0:T(8,128)(2,1)S(1)} %get-tuple-element.12.d_t, bf16[1024,128]{1,0:T(8,128)(2,1)S(1)} %get-tuple-element.13.dip, ...), custom_call_target="tpu_custom_call" | custom-call | tf_op jit(solution)/shard_map/store/pallas_call | solution.py:476

commit v6 on v4

--- a/solution.py
+++ b/solution.py
@@ -19,8 +19,8 @@
 TILE = 128
 PER = TILE // ROWS
 AHEAD = 5
-LAG_SUM = 1
-LAG_OWN = 6
+LAG_SUM = 3
+LAG_OWN = 7
 STAGES = (3, 4, 5)
 BLOCK = 256
 LANE = 128

time: 152 us -> 152 us (level)
  no operation moved by 1% of the time
where the time goes in v6:
time: 152 us
  Pallas kernels  151 us (99%)
    pallas_call x1, Pallas kernels, on_device(): pl.pallas_call(body, out_shape=(pltpu.VMEM((NORB, NORB), F32), pltpu.VMEM...  149 us

profile of v6, /device:TPU:40, one launch (start us, length us, event | category | flops | bytes accessed | tf_op | source)
XLA Modules:
  0.0 152.3 jit_solution(11536406831160326941)
XLA Ops:
  1.3 148.9 %stencil.1 = (f32[1024,1024]{1,0:T(8,128)S(1)}, bf16[128,1024]{1,0:T(8,128)(2,1)S(1)}, bf16[1024,1024]{1,0:T(8,128)(2,1)S(1)}, bf16[1024,128]{1,0:T(8,128)(2,1)S...) custom-call(bf16[2,1024,1024]{2,1,0:T(8,128)(2,1)} %bitcast.6, f32[8,128]{1,0:T(8,128)} %bitcast.9, ...), custom_call_target="tpu_custom_call" | custom-call | flops 8589934592 | bytes 10485760 | tf_op jit(solution)/shard_map/stencil/pallas_call | solution.py:424
  150.2 2.1 %store.1 = (bf16[2,1024,1024]{2,1,0:T(8,128)(2,1)}, f32[8,128]{1,0:T(8,128)}) custom-call(f32[1024,1024]{1,0:T(8,128)S(1)} %get-tuple-element.10.total, bf16[128,1024]{1,0:T(8,128)(2,1)S(1)} %get-tuple-element.11.mixed, bf16[1024,1024]{1,0:T(8,128)(2,1)S(1)} %get-tuple-element.12.d_t, bf16[1024,128]{1,0:T(8,128)(2,1)S(1)} %get-tuple-element.13.dip, ...), custom_call_target="tpu_custom_call" | custom-call | tf_op jit(solution)/shard_map/store/pallas_call | solution.py:472
